TPU v7x, 256 devices: a whole 4x4x8 slice. The times are simulated.
256 devices in a mesh: wide: 32 (over z, y), seq: 8 (over x, core).
Axes of the slice: x: 4, y: 4, z: 8, core: 2. Of those that a mesh axis runs over, the one named last changes fastest.
Arguments:
- queries: bfloat16 [65536, 6144], P(('wide', 'seq')), may hold values from -20 to 20
- keys: bfloat16 [65536, 6144], P(('wide', 'seq')), may hold values from -20 to 20
- values: bfloat16 [65536, 6144], P(('wide', 'seq')), may hold values from -6 to 6
- spatial_mask: int32 [48, 32, 16, 16], P(None, 'wide'), may hold values from 0 to 1, as said below
- temporal_mask: int32 [48, 16, 32, 32], P(None, None, 'wide'), may hold values from 0 to 1, as said below
Outputs:
- attended: bfloat16 [65536, 6144], P(('wide', 'seq'))
Inputs may be any that keep to these rules, and one draw needn't show every extreme that they name: Every row of spatial_mask has 1 to 3 ones and always includes its own block; some row has exactly 3. Every row of temporal_mask has at most 2 ones and never names its own frame; some row has exactly 2.
All inputs are finite; a program needn't handle non-finite values.
Results may differ from a plain program's by a relative error of at most 0.014.
Values may be sent and summed in bfloat16 or wider, within the bound.
A program may use at most 192 MiB of HBM per device.

v0:
```python
import jax
import jax.numpy as jnp
from jax import lax
from jax.sharding import PartitionSpec as P

SMAX = 3
TMAX = 2


NEG = -1e30


def block_lists(mask, slots):
    columns_total = mask.shape[-1]
    position = jnp.cumsum(mask, axis=-1) - 1
    places = jnp.arange(slots, dtype=jnp.int32)
    chosen = (mask[..., None, :] == 1) & (position[..., None, :] == places[:, None])
    columns = jnp.arange(columns_total, dtype=jnp.int32)
    block_index = jnp.sum(jnp.where(chosen, columns, 0), axis=-1)
    block_count = jnp.sum(mask, axis=-1)
    return (block_index, block_count)


def attend(query_rows, key_rows, value_rows, flat_index, block_count, score_scale):
    row_count, block_width, head_dim = query_rows.shape
    start_state = (
        jnp.full((row_count, block_width), NEG, jnp.float32),
        jnp.zeros((row_count, block_width), jnp.float32),
        jnp.zeros((row_count, block_width, head_dim), jnp.float32),
    )

    def visit_slot(slot_index, state):
        running_max, running_sum, running_out = state
        target = lax.dynamic_index_in_dim(flat_index, slot_index, 1, keepdims=False)
        live_rows = (slot_index < block_count)[:, None, None]
        key_block = jnp.take(key_rows, target, axis=0)
        value_block = jnp.take(value_rows, target, axis=0)
        scores = (
            jnp.einsum("nqd,nkd->nqk", query_rows, key_block, preferred_element_type=jnp.float32)
            * score_scale
        )
        scores = jnp.where(live_rows, scores, NEG)
        newest = jnp.maximum(running_max, jnp.max(scores, axis=-1))
        weights = jnp.where(live_rows, jnp.exp(scores - newest[..., None]), 0.0)
        factor = jnp.exp(running_max - newest)
        running_sum = running_sum * factor + jnp.sum(weights, axis=-1)
        running_out = running_out * factor[..., None] + jnp.einsum(
            "nqk,nkd->nqd",
            weights.astype(jnp.bfloat16),
            value_block,
            preferred_element_type=jnp.float32,
        )
        return (newest, running_sum, running_out)

    return lax.fori_loop(0, jnp.max(block_count), visit_slot, start_state)


def combine(local_part, remote_part):
    highest = jnp.maximum(local_part[1], remote_part[1])
    local_factor = jnp.exp(local_part[1] - highest)
    remote_factor = jnp.exp(remote_part[1] - highest)
    numerator = local_part[0] * local_factor[..., None] + remote_part[0] * remote_factor[..., None]
    denominator = local_part[2] * local_factor + remote_part[2] * remote_factor
    return (numerator / denominator[..., None]).astype(jnp.bfloat16)


def pack_outgoing(members, mask_rows, head_dim):
    wide_count, pair_count, single, frames = mask_rows.shape
    mask_lines = -(-frames // head_dim)
    padded = jnp.pad(
        mask_rows.astype(jnp.bfloat16),
        ((0, 0), (0, 0), (0, 0), (0, mask_lines * head_dim - frames)),
    )
    padded = padded.reshape(wide_count, pair_count, single, mask_lines, head_dim)
    return jnp.concatenate(list(members) + [padded], axis=3)


def split_returned(returned, head_dim):
    return (returned[..., :head_dim], returned[..., head_dim], returned[..., head_dim + 1])


def per_device(queries, keys, values, spatial_mask, temporal_mask):
    tok_rows = queries.shape[0]
    head_total = spatial_mask.shape[0]
    head_dim = queries.shape[1] // head_total
    blocks = spatial_mask.shape[2]
    frames = temporal_mask.shape[3]
    wide_count = lax.axis_size("wide")
    seq_count = lax.axis_size("seq")
    local_heads = head_total // seq_count
    block_rows = tok_rows * seq_count // blocks
    score_scale = head_dim ** (-0.5)
    stacked = (
        queries.reshape(tok_rows, head_total, head_dim),
        keys.reshape(tok_rows, head_total, head_dim),
        values.reshape(tok_rows, head_total, head_dim),
    )
    by_heads = (
        lax.all_to_all(stacked[0], "seq", split_axis=1, concat_axis=0, tiled=True),
        lax.all_to_all(stacked[1], "seq", split_axis=1, concat_axis=0, tiled=True),
        lax.all_to_all(stacked[2], "seq", split_axis=1, concat_axis=0, tiled=True),
    )
    layout = tuple(
        (
            jnp.transpose(member.reshape(blocks, block_rows, local_heads, head_dim), (2, 0, 1, 3))
            for member in by_heads
        )
    )
    head_start = lax.axis_index("seq") * local_heads
    own_spatial = lax.dynamic_slice_in_dim(spatial_mask, head_start, local_heads, 0).reshape(
        local_heads, blocks, blocks
    )
    spatial_index, spatial_count = block_lists(own_spatial, SMAX)
    spatial_flat = (
        spatial_index + (jnp.arange(local_heads, dtype=jnp.int32) * blocks)[:, None, None]
    )
    row_shape = (local_heads * blocks, block_rows, head_dim)
    spatial_state = attend(
        layout[0].reshape(row_shape),
        layout[1].reshape(row_shape),
        layout[2].reshape(row_shape),
        spatial_flat.reshape(local_heads * blocks, SMAX),
        spatial_count.reshape(-1),
        score_scale,
    )
    pair_count = local_heads * blocks // wide_count
    own_temporal = lax.dynamic_slice_in_dim(temporal_mask, head_start, local_heads, 0)
    members = tuple(
        (member.reshape(wide_count, pair_count, 1, block_rows, head_dim) for member in layout)
    )
    outgoing = pack_outgoing(
        members, own_temporal.reshape(wide_count, pair_count, 1, frames), head_dim
    )
    incoming = lax.all_to_all(outgoing, "wide", split_axis=0, concat_axis=2, tiled=True)
    pair_total = incoming.shape[1]
    pair_shape = (pair_total * frames, block_rows, head_dim)
    query_in = incoming[0, :, :, :block_rows]
    key_in = incoming[0, :, :, block_rows : 2 * block_rows]
    value_in = incoming[0, :, :, 2 * block_rows : 3 * block_rows]
    mask_in = incoming[0, :, :, 3 * block_rows :].reshape(pair_total, frames, -1)[..., :frames]
    live_mask = (mask_in > 0).astype(jnp.int32)
    block_index, block_count = block_lists(live_mask, TMAX)
    flat_index = block_index + (jnp.arange(pair_total, dtype=jnp.int32) * frames)[:, None, None]
    running_max, running_sum, running_out = attend(
        query_in.reshape(pair_shape),
        key_in.reshape(pair_shape),
        value_in.reshape(pair_shape),
        flat_index.reshape(pair_total * frames, TMAX),
        block_count.reshape(-1),
        score_scale,
    )
    joined = jnp.concatenate([running_out, running_max[..., None], running_sum[..., None]], axis=-1)
    partial_value = joined.reshape(1, pair_total, frames, block_rows, head_dim + 2)
    returned = lax.all_to_all(
        partial_value.astype(jnp.bfloat16), "wide", split_axis=2, concat_axis=0, tiled=True
    ).astype(partial_value.dtype)
    remote_out, remote_max, remote_sum = split_returned(returned, head_dim)
    remote_part = (
        remote_out.reshape(local_heads, blocks, block_rows, head_dim),
        remote_max.reshape(local_heads, blocks, block_rows),
        remote_sum.reshape(local_heads, blocks, block_rows),
    )
    local_part = (
        spatial_state[2].reshape(local_heads, blocks, block_rows, head_dim),
        spatial_state[0].reshape(local_heads, blocks, block_rows),
        spatial_state[1].reshape(local_heads, blocks, block_rows),
    )
    merged = combine(local_part, remote_part)
    leaving = jnp.transpose(merged, (1, 2, 0, 3)).reshape(
        blocks * block_rows, local_heads, head_dim
    )
    result = lax.all_to_all(leaving, "seq", split_axis=0, concat_axis=1, tiled=True)
    return result.reshape(tok_rows, head_total * head_dim)


def solution(mesh):
    return jax.shard_map(
        per_device,
        mesh=mesh,
        in_specs=(
            P(("wide", "seq"), None),
            P(("wide", "seq"), None),
            P(("wide", "seq"), None),
            P(None, "wide", None, None),
            P(None, None, "wide", None),
        ),
        out_specs=P(("wide", "seq"), None),
        check_vma=False,
    )
```

profile of v0, /device:TPU:32, one launch (start us, length us, event | category | flops | bytes accessed | tf_op | source)
XLA Modules:
  0.0 677.9 jit_solution(4152951721904597607)
XLA Ops:
  0.0 4.7 copy.158
  4.7 4.3 all-to-all-start.1
  9.0 4.7 copy.155
  13.7 33.7 %all-to-all-done.1 = bf16[256,48,128]{0,2,1:T(8,128)(2,1)S(1)} async-done(((bf16[256,48,128]{0,2,1:T(8,128)(2,1)}), bf16[256,48,128]{0,2,1:T(8,128)(2,1)S(1)}, u32[]{:S(2)}, u32[]{:S(2)}) %all-to-all-start.1) | async-done | bytes 3145760 | tf_op jit(solution)/shard_map/all_to_all | solution.py:99
  47.4 4.4 all-to-all-start
  51.9 4.6 copy.161
  56.5 33.8 %all-to-all-done = bf16[256,48,128]{0,2,1:T(8,128)(2,1)} async-done(((bf16[256,48,128]{0,2,1:T(8,128)(2,1)}), bf16[256,48,128]{0,2,1:T(8,128)(2,1)}, u32[]{:S(2)}, u32[]{:S(2)}) %all-to-all-start) | async-done | bytes 3145760 | tf_op jit(solution)/shard_map/all_to_all | solution.py:100
  90.3 4.4 all-to-all-start.2
  99.7 3.5 copy.157
  103.2 30.0 %all-to-all-done.2 = bf16[256,48,128]{0,2,1:T(8,128)(2,1)} async-done(((bf16[256,48,128]{0,2,1:T(8,128)(2,1)}), bf16[256,48,128]{0,2,1:T(8,128)(2,1)}, u32[]{:S(2)}, u32[]{:S(2)}) %all-to-all-start.2) | async-done | bytes 3145760 | tf_op jit(solution)/shard_map/all_to_all | solution.py:101
  133.2 4.6 copy.163
  137.8 8.0 %maximum_bitcast_fusion = bf16[32,3,1,385,128]{4,3,1,2,0:T(8,128)(2,1)} fusion(bf16[32,3,1,1,128]{4,3,1,0,2:T(2,128)(2,1)S(1)} %copy.166, bf16[32,3,1,128,128]{4,3,1,0,2:T(8,128)(2,1)} %bitcast.135, bf16[32,3,1,128,128]{4,3,1,0,2:T(8,128)(2,1)S(1)} %bitcast.133, bf16[32,3,1,128,128]{4,3,1,0,2:T(8,128)(2,1)} %bitcast.149), kind=kLoop, calls=%fused_computation.71 | loop fusion | flops 37847040 | bytes 18923520 | tf_op jit(solution)/shard_map/concatenate | solution.py:75
  145.8 11.5 %all-to-all-start.3 = ((bf16[32,3,1,385,128]{4,3,1,2,0:T(8,128)(2,1)}), bf16[32,3,1,385,128]{4,3,1,2,0:T(8,128)(2,1)}, u32[]{:S(2)}, u32[]{:S(2)}) async-start(bf16[32,3,1,385,128]{4,3,1,2,0:T(8,128)(2,1)} %maximum_bitcast_fusion), calls=%async_computation.3 | async-start | bytes 19267584 | tf_op jit(solution)/shard_map/all_to_all | solution.py:134
  160.3 211.3 %all-to-all-done.3 = bf16[32,3,1,385,128]{4,3,1,2,0:T(8,128)(2,1)} async-done(((bf16[32,3,1,385,128]{4,3,1,2,0:T(8,128)(2,1)}), bf16[32,3,1,385,128]{4,3,1,2,0:T(8,128)(2,1)}, u32[]{:S(2)}, u32[]{:S(2)}) %all-to-all-start.3) | async-done | bytes 9461792 | tf_op jit(solution)/shard_map/all_to_all | solution.py:134
  371.7 8.9 %copy.194 = bf16[32,3,1,385,128]{4,0,1,3,2:T(8,128)(2,1)} copy(bf16[32,3,1,385,128]{4,3,1,2,0:T(8,128)(2,1)} %all-to-all-done.3) | data formatting | bytes 18923520 | tf_op jit(solution)/shard_map/all_to_all | solution.py:134
  381.3 6.5 fusion.64
  388.7 4.8 copy.172
  394.3 4.7 copy.171
  402.0 3.4 broadcast.83.clone
  405.4 25.1 %while.29 = (s32[]{:T(128)}, f32[96,128]{1,0:T(8,128)S(1)}, f32[96,128]{1,0:T(8,128)S(1)}, f32[96,128,128]{2,1,0:T(8,128)}, s32[]{:T(128)}, /*index=5*/s32[96]{0...) while((s32[]{:T(128)}, f32[96,128]{1,0:T(8,128)S(1)}, ...), condition=%wide.region_15.17_spmd, body=%wide.region_12.16_spmd.sunk | while | flops 832071296 | bytes 54271056 | solution.py:55
  409.6 4.6 gather_fusion.2
  414.2 5.2 bitcast_reduce_fusion.5
  421.2 8.7 %multiply_add_fusion.12 = f32[96,128,128]{2,1,0:T(8,128)} fusion(f32[96,128,128]{2,1,0:T(8,128)} %get-tuple-element.356, f32[96,128]{1,0:T(8,128)S(1)} %get-tuple-element.339, bf16[96,128,128]{2,1,0:T(8,128)(2,1)S(1)} %gather_fusion.3, pred[96]{0:T(512)(128)(4,1)S(1)} %get-tuple-element.335, f32[96,128,128]{2,1,0:T(8,128)S(1)} %get-tuple-element.337, ...), kind=kOutput, calls=%fused_computation.41.clone.1 | convolution fusion | flops 415236096 | bytes 22118592 | tf_op jit(solution)/shard_map/while/body/nqk,nkd->nqd/dot_general | solution.py:47
  430.6 5.2 convert.15
  440.1 8.0 %pad_maximum_fusion = bf16[1,3,32,128,130]{4,3,2,1,0:T(8,128)(2,1)} fusion(bf16[1,3,32,128,1]{4,3,2,1,0:T(8,128)(2,1)S(1)} %copy.174, bf16[1,3,32,128,1]{4,3,2,1,0:T(8,128)(2,1)} %copy.173, bf16[1,3,32,128,128]{4,3,2,1,0:T(8,128)(2,1)} %bitcast.151), kind=kLoop, calls=%fused_computation.75 | loop fusion | flops 9584640 | bytes 6389760 | tf_op jit(solution)/shard_map/concatenate | solution.py:152
  448.2 7.5 %copy.175 = bf16[1,3,32,128,130]{3,4,1,0,2:T(8,128)(2,1)} copy(bf16[1,3,32,128,130]{4,3,2,1,0:T(8,128)(2,1)} %pad_maximum_fusion) | data formatting | bytes 6389760 | tf_op jit(solution)/shard_map/concatenate | solution.py:152
  455.7 37.3 %all-to-all-start.4 = ((bf16[1,3,32,128,130]{3,4,1,0,2:T(8,128)(2,1)}), bf16[1,3,32,128,130]{3,4,1,0,2:T(8,128)(2,1)}, u32[]{:S(2)}, u32[]{:S(2)}) async-start(bf16[1,3,32,128,130]{3,4,1,0,2:T(8,128)(2,1)} %copy.175), calls=%async_computation.4 | async-start | bytes 6684672 | tf_op jit(solution)/shard_map/all_to_all | solution.py:154
  493.1 3.4 broadcast.83.clone.1
  496.5 72.7 %while.28 = (s32[]{:T(128)}, f32[96,128]{1,0:T(8,128)S(1)}, f32[96,128]{1,0:T(8,128)S(1)}, f32[96,128,128]{2,1,0:T(8,128)}, s32[]{:T(128)}, /*index=5*/s32[96]{0...) while((s32[]{:T(128)}, f32[96,128]{1,0:T(8,128)S(1)}, ...), condition=%wide.region_7.9_spmd, body=%wide.region_4.8_spmd.sunk | while | flops 832071296 | bytes 54271056 | solution.py:55
  497.3 3.0 gather_fusion.1
  500.4 4.6 gather_fusion
  504.9 5.2 bitcast_reduce_fusion.4
  512.0 8.7 %multiply_add_fusion.10 = f32[96,128,128]{2,1,0:T(8,128)} fusion(f32[96,128,128]{2,1,0:T(8,128)} %get-tuple-element.395, f32[96,128]{1,0:T(8,128)S(1)} %get-tuple-element.322, bf16[96,128,128]{2,1,0:T(8,128)(2,1)S(1)} %gather_fusion.1, pred[96]{0:T(512)(128)(4,1)S(1)} %get-tuple-element.318, f32[96,128,128]{2,1,0:T(8,128)S(1)} %get-tuple-element.320, ...), kind=kOutput, calls=%fused_computation.8.clone.1 | convolution fusion | flops 415236096 | bytes 22118592 | tf_op jit(solution)/shard_map/while/body/nqk,nkd->nqd/dot_general | solution.py:47
  521.3 3.0 gather_fusion.1
  524.4 4.6 gather_fusion
  528.9 5.2 bitcast_reduce_fusion.4
  536.0 8.7 %multiply_add_fusion.10 = f32[96,128,128]{2,1,0:T(8,128)} fusion(f32[96,128,128]{2,1,0:T(8,128)} %get-tuple-element.395, f32[96,128]{1,0:T(8,128)S(1)} %get-tuple-element.322, bf16[96,128,128]{2,1,0:T(8,128)(2,1)S(1)} %gather_fusion.1, pred[96]{0:T(512)(128)(4,1)S(1)} %get-tuple-element.318, f32[96,128,128]{2,1,0:T(8,128)S(1)} %get-tuple-element.320, ...), kind=kOutput, calls=%fused_computation.8.clone.1 | convolution fusion | flops 415236096 | bytes 22118592 | tf_op jit(solution)/shard_map/while/body/nqk,nkd->nqd/dot_general | solution.py:47
  548.4 4.6 gather_fusion
  552.9 5.2 bitcast_reduce_fusion.4
  560.0 8.7 %multiply_add_fusion.10 = f32[96,128,128]{2,1,0:T(8,128)} fusion(f32[96,128,128]{2,1,0:T(8,128)} %get-tuple-element.395, f32[96,128]{1,0:T(8,128)S(1)} %get-tuple-element.322, bf16[96,128,128]{2,1,0:T(8,128)(2,1)S(1)} %gather_fusion.1, pred[96]{0:T(512)(128)(4,1)S(1)} %get-tuple-element.318, f32[96,128,128]{2,1,0:T(8,128)S(1)} %get-tuple-element.320, ...), kind=kOutput, calls=%fused_computation.8.clone.1 | convolution fusion | flops 415236096 | bytes 22118592 | tf_op jit(solution)/shard_map/while/body/nqk,nkd->nqd/dot_general | solution.py:47
  569.3 7.3 %copy.176 = bf16[1,3,32,128,130]{4,3,1,2,0:T(8,128)(2,1)} copy(bf16[1,3,32,128,130]{3,4,1,0,2:T(8,128)(2,1)} %all-to-all-done.4) | data formatting | bytes 6389760 | tf_op jit(solution)/shard_map/all_to_all | solution.py:154
  576.5 4.6 convert_bitcast_fusion
  581.2 5.1 slice_reduce_fusion.1
  586.2 3.3 slice.46
  589.6 7.2 %divide_convert_fusion = bf16[6,16,128,128]{3,2,1,0:T(8,128)(2,1)S(1)} fusion(f32[6,16,128,128]{3,2,1,0:T(8,128)} %bitcast.141, f32[6,16,128,128]{3,2,1,0:T(8,128)} %bitcast.132, f32[6,16,128]{2,1,0:T(8,128)S(1)} %get-tuple-element.172, f32[6,16,128]{2,1,0:T(8,128)S(1)} %get-tuple-element.174, f32[6,16,128]{2,1,0:T(8,128)S(1)} %get-tuple-element.173), kind=kLoop, calls=%fused_computation.76 | loop fusion | flops 7864320 | bytes 15876096 | tf_op jit(solution)/shard_map/convert_element_type | solution.py:64
  596.8 12.1 %copy.177 = bf16[2048,6,128]{2,1,0:T(8,128)(2,1)S(1)} copy(bf16[2048,6,128]{2,0,1:T(8,128)(2,1)S(1)} %bitcast.148) | data formatting | bytes 6291456 | tf_op jit(solution)/shard_map/reshape | solution.py:169
  608.9 60.0 %all_to_all.87 = bf16[2048,6,128]{2,1,0:T(8,128)(2,1)} all-to-all(bf16[2048,6,128]{2,1,0:T(8,128)(2,1)S(1)} %copy.177), channel_id=1, replica_groups=mesh['wide'=32,'seq'=8] {'seq'}, dimensions={0} | all-to-all | bytes 6291456 | tf_op jit(solution)/shard_map/all_to_all | solution.py:172
  668.9 5.8 copy.179
  (84 shorter events, 34.1 us)
Async XLA Ops:
  0.0 94.8 %copy-start = (s32[48,16,1,32]{0,3,2,1:T(8,128)S(1)}, s32[48,16,1,32]{0,3,2,1:T(8,128)}, u32[]{:S(2)}) copy-start(s32[48,16,1,32]{0,3,2,1:T(8,128)} %param.15) | copy-start | bytes 294916
  4.7 42.7 %all-to-all-start.1 = ((bf16[256,48,128]{0,2,1:T(8,128)(2,1)}), bf16[256,48,128]{0,2,1:T(8,128)(2,1)S(1)}, u32[]{:S(2)}, u32[]{:S(2)}) async-start(bf16[256,48,128]{0,2,1:T(8,128)(2,1)} %bitcast.147), calls=%async_computation.1 | async-start | bytes 6291456 | tf_op jit(solution)/shard_map/all_to_all | solution.py:99
  47.4 42.9 %all-to-all-start = ((bf16[256,48,128]{0,2,1:T(8,128)(2,1)}), bf16[256,48,128]{0,2,1:T(8,128)(2,1)}, u32[]{:S(2)}, u32[]{:S(2)}) async-start(bf16[256,48,128]{0,2,1:T(8,128)(2,1)} %bitcast.146), calls=%async_computation | async-start | bytes 6291456 | tf_op jit(solution)/shard_map/all_to_all | solution.py:100
  90.3 42.9 %all-to-all-start.2 = ((bf16[256,48,128]{0,2,1:T(8,128)(2,1)}), bf16[256,48,128]{0,2,1:T(8,128)(2,1)}, u32[]{:S(2)}, u32[]{:S(2)}) async-start(bf16[256,48,128]{0,2,1:T(8,128)(2,1)} %bitcast.145), calls=%async_computation.2 | async-start | bytes 6291456 | tf_op jit(solution)/shard_map/all_to_all | solution.py:101
  103.2 42.6 %copy-start.2 = (bf16[8,256,6,128]{3,1,0,2:T(8,128)(2,1)}, bf16[8,256,6,128]{3,1,0,2:T(8,128)(2,1)S(1)}, u32[]{:S(2)}) copy-start(bf16[8,256,6,128]{3,1,0,2:T(8,128)(2,1)S(1)} %copy.157) | copy-start | bytes 9437188
  145.8 11.9 %copy-start.3 = (s32[48,1,16,16]{0,3,2,1:T(8,128)S(1)}, s32[48,1,16,16]{0,3,2,1:T(8,128)}, u32[]{:S(2)}) copy-start(s32[48,1,16,16]{0,3,2,1:T(8,128)} %param.14) | copy-start | bytes 147460
  145.8 225.9 %all-to-all-start.3 = ((bf16[32,3,1,385,128]{4,3,1,2,0:T(8,128)(2,1)}), bf16[32,3,1,385,128]{4,3,1,2,0:T(8,128)(2,1)}, u32[]{:S(2)}, u32[]{:S(2)}) async-start(bf16[32,3,1,385,128]{4,3,1,2,0:T(8,128)(2,1)} %maximum_bitcast_fusion), calls=%async_computation.3 | async-start | bytes 19267584 | tf_op jit(solution)/shard_map/all_to_all | solution.py:134
  455.7 113.6 %all-to-all-start.4 = ((bf16[1,3,32,128,130]{3,4,1,0,2:T(8,128)(2,1)}), bf16[1,3,32,128,130]{3,4,1,0,2:T(8,128)(2,1)}, u32[]{:S(2)}, u32[]{:S(2)}) async-start(bf16[1,3,32,128,130]{3,4,1,0,2:T(8,128)(2,1)} %copy.175), calls=%async_computation.4 | async-start | bytes 6684672 | tf_op jit(solution)/shard_map/all_to_all | solution.py:154
  668.9 8.8 %copy-start.1 = (s32[48,16,1,32]{0,3,2,1:T(8,128)S(1)}, s32[48,16,1,32]{0,3,2,1:T(8,128)}, u32[]{:S(2)}) copy-start(s32[48,16,1,32]{0,3,2,1:T(8,128)} %param.15) | copy-start | bytes 294916
where the time goes:
time: 689 us; the launch traced here: 678 us
  waiting for transfers between devices  309 us (45%)
  local copies, waits for them, and re-layouts  142 us (21%)
  starting transfers between devices  62.1 us (9%)
  blocking collectives  60 us (9%)
  matrix products  55.7 us (8%)
  other arithmetic  44.1 us (6%)
    all_to_all x1, waiting for transfers between devices, per_device(): lax.all_to_all(outgoing, 'wide', split_axis=0, concat_axis=2, tiled=True)  211 us
    all_to_all x1, blocking collectives, per_device(): lax.all_to_all(leaving, 'seq', split_axis=0, concat_axis=1, tiled=True)  60 us
    all_to_all x1, starting transfers between devices, per_device(): lax.all_to_all(partial_value.astype(jnp.bfloat16), 'wide', split_axis=2,...  37.3 us
    dot_general x4, matrix products, visit_slot(): jnp.einsum('nqk,nkd->nqd', weights.astype(jnp.bfloat16), value_block, pre...  34.9 us
    all_to_all x1, waiting for transfers between devices, per_device(): lax.all_to_all(stacked[1], 'seq', split_axis=1, concat_axis=0, tiled=True)  33.8 us
    all_to_all x1, waiting for transfers between devices, per_device(): lax.all_to_all(stacked[0], 'seq', split_axis=1, concat_axis=0, tiled=True)  33.7 us
    all_to_all x1, waiting for transfers between devices, per_device(): lax.all_to_all(stacked[2], 'seq', split_axis=1, concat_axis=0, tiled=True)  30 us
    dot_general x4, matrix products, visit_slot(): jnp.einsum('nqd,nkd->nqk', query_rows, key_block, preferred_element_type=...  20.8 us
  transfers between devices with their start and end apart: 5, of which 4 were waited for; matrix products, arithmetic and copies ran while one was open for 14% of the time, Pallas kernels for 0%

commit v1 on v0

v1 whole, which is shorter than its diff:
```python
import functools
import math

import jax
import jax.numpy as jnp
from jax import lax
from jax.experimental import pallas as pl
from jax.experimental.pallas import tpu as pltpu
from jax.sharding import PartitionSpec as P

MESH = pl.DeviceIdType.MESH
BLK = 128
DEAD = -1e30
CODE = 64
UNROLL = 2


def kernel(cfg, q_ref, k_ref, v_ref, tm_ref, sm_ref, out_ref, *scratch):
    W, S, H, NP, C2, NZ, NY = cfg
    BPF = 2 * S
    scratch = list(scratch)

    def take(n):
        got = scratch[:n]
        del scratch[:n]
        return got

    inputs = (k_ref, v_ref, q_ref)
    t_in = [take(3) for _ in range(NP)]
    s_in = [take(3) for _ in range(NP)]
    t_out, s_out, t_got, s_got, t_lse, s_lse, t_lgot, s_lgot, out_v = (take(NP) for _ in range(9))
    tm_v, sm_v, own_v, tl_v, sl_v, tl_s, sl_s = take(7)
    t_recv, s_recv, t_send, s_send, o_recv, o_send, l_recv, l_send, list_sem, out_sem, last_o, last_l, last_q = take(13)

    wide, seq = lax.axis_index("wide"), lax.axis_index("seq")
    my_z, my_y = wide // NY, wide % NY
    scale = math.log2(math.e) * BLK ** -0.5

    def frame_at(i):
        zi, dy = i % NZ, i // NZ
        half = (zi + 1) // 2
        dz = half + (zi + 1) % 2 * (NZ - 2 * half)
        return (my_z + dz) % NZ * NY + (my_y + dy) % NY

    def column(h):
        return pl.ds(pl.multiple_of(h * BLK, BLK), BLK)

    def at(dz, dy):
        return (my_z + dz) % NZ * NY + (my_y + dy) % NY

    def wait_all(ref, sem):
        pltpu.make_async_copy(ref, ref, sem).wait()

    pltpu.make_async_copy(tm_ref.at[pl.ds(2 * seq, 2)], tm_v, list_sem.at[2]).start()
    pltpu.make_async_copy(sm_ref.at[0], sm_v, list_sem.at[3]).start()

    barrier = pltpu.get_barrier_semaphore()

    def greet_wide(i, _):
        pl.semaphore_signal(barrier, inc=1, device_id=(frame_at(i), seq), device_id_type=MESH)
        return 0

    def greet_seq(i, _):
        pl.semaphore_signal(barrier, inc=1, device_id=(wide, (seq + i) % S), device_id_type=MESH)
        return 0

    lax.fori_loop(1, W, greet_wide, 0)
    lax.fori_loop(1, S, greet_seq, 0)
    pl.semaphore_wait(barrier, W - 1 + S - 1)

    def remote(src, dst, send, recv, device):
        return pltpu.make_async_remote_copy(
            src_ref=src, dst_ref=dst, send_sem=send, recv_sem=recv, device_id=device, device_id_type=MESH
        )

    def coded(mask):
        last = mask.shape[0] - 1
        places = lax.broadcasted_iota(jnp.int32, mask.shape, 0)
        high = jnp.max(places * mask, axis=0, keepdims=True)
        low = last - jnp.max((last - places) * mask, axis=0, keepdims=True)
        count = jnp.sum(mask, axis=0, keepdims=True)
        return low, high, count

    def encode(low, high, count):
        return low + CODE * high + CODE * CODE * count

    def decode(code):
        return code % CODE, code // CODE % CODE, code // (CODE * CODE)

    def send_lists(i, _):
        to = frame_at(i)
        remote(own_v.at[place_of(to, 0)[1]], tl_v.at[wide], list_sem.at[1], list_sem.at[0], (to, seq)).start()
        return 0

    def place_of(worker, p):
        pair = NP * worker + p
        return pair % H, pair // H

    def source(n, place):
        head, block = place
        return inputs[n].at[block, :, column(head)]

    def send_pairs(p, dz, dy, n, arrived):
        to = at(dz, dy)
        remote(
            source(n, place_of(to, p)), t_in[p][n].at[wide], t_send.at[p, n], arrived, (to, seq)
        ).start()

    def two_ways(g, dy):
        last = (g + 1) // half
        return (g + 1, dy), ((NZ - g - 1) * (1 - last), (NY - dy) % NY), (last == 1) & (dy == 0)

    def walk(j):
        k, g = j // half, j % half
        return g, (g + k) % NY

    def group_there(g, dy):
        last = (g + 1) // half
        return (dy * (1 - 2 * last) - g + NY * NZ) % NY

    def send_both_ways(p, j, n, arrived=None):
        g, dy = walk(j)
        if arrived is None:
            arrived = last_q.at[group_there(g, dy)]
        ahead, back, mine = two_ways(g, dy)
        send_pairs(p, *ahead, n, arrived)

        @pl.when(jnp.logical_not(mine))
        def _():
            send_pairs(p, *back, n, arrived)

    def send_heads(p, j, n):
        to, c2 = (seq + 1 + j // C2) % S, j % C2
        remote(
            inputs[n].at[:, :, column(to * (NP * C2) + p + NP * c2)],
            s_in[p][n].at[pl.ds(c2 * BPF + 2 * seq, 2)],
            s_send.at[p, n],
            s_recv.at[p, n],
            (wide, to),
        ).start()

    head_sends = C2 * (S - 1)
    half = NZ // 2
    steps = NY * half
    assert head_sends <= steps and NP == 3

    def some_heads(p, j, n, first, count):
        @pl.when((j >= first) & (j < first + count))
        def _():
            send_heads(p, j - first + (head_sends - count if first == 0 else 0), n)

    early = head_sends // 2
    for p in range(NP):
        for n in range(3 if p < NP - 1 else 2):

            def both(j, _, p=p, n=n):
                send_both_ways(p, j, n, t_recv.at[p, n])
                if p == 0:
                    some_heads(0, j, n, 0, head_sends)
                    some_heads(1, j, n, steps - early, early)
                elif p == 1:
                    some_heads(1, j, n, 0, head_sends - early)
                    some_heads(2, j, n, steps - head_sends, head_sends)
                return 0

            lax.fori_loop(0, steps, both, 0)
        for n in range(3):
            own = source(n, place_of(wide, p))
            arrived = last_q.at[group_there(half - 1, 0)] if p == NP - 1 and n == 2 else t_recv.at[p, n]
            pltpu.make_async_copy(own, t_in[p][n].at[wide], arrived).start()
            for c2 in range(C2):
                pltpu.make_async_copy(
                    inputs[n].at[:, :, column(seq * (NP * C2) + p + NP * c2)],
                    s_in[p][n].at[pl.ds(c2 * BPF + 2 * seq, 2)],
                    s_recv.at[p, n],
                ).start()
        if p == 0:
            wait_all(tm_v, list_sem.at[2])
            for block in range(2):
                low, high, count = coded(tm_v[block, 0])
                none = count == 0
                own_v[block] = encode(jnp.where(none, 0, low), jnp.where(none, 0, high), count)
            pltpu.make_async_copy(own_v.at[place_of(wide, 0)[1]], tl_v.at[wide], list_sem.at[0]).start()
            lax.fori_loop(1, W, send_lists, 0)

    def last_queries(j, _):
        send_both_ways(NP - 1, j, 2)
        return 0

    lax.fori_loop(0, steps, last_queries, 0)

    wait_all(sm_v, list_sem.at[3])
    for block in range(BPF):
        mask = sm_v[block]
        others = jnp.where(lax.broadcasted_iota(jnp.int32, mask.shape, 0) == block, 0, mask)
        low, high, count = coded(others)
        none = count == 0
        sl_v[block] = encode(jnp.where(none, block, low), jnp.where(none, block, high), count)
    space_lists = pltpu.make_async_copy(sl_v, sl_s, list_sem.at[2])
    space_lists.start()
    space_lists.wait()

    wait_all(tl_v, list_sem.at[0])
    time_lists = pltpu.make_async_copy(tl_v, tl_s, list_sem.at[2])
    time_lists.start()
    time_lists.wait()

    row_id = lax.broadcasted_iota(jnp.int32, (BLK, BLK), 0)
    col_id = lax.broadcasted_iota(jnp.int32, (BLK, BLK), 1)
    eye = row_id == col_id

    def attend(query, keys, values, biases):
        key_all = jnp.concatenate(keys, axis=0)
        scores = lax.dot_general(query, key_all, (((1,), (1,)), ((), ())), preferred_element_type=jnp.float32)
        top = jnp.max(scores, axis=1, keepdims=True)
        if biases is None:
            weights = jnp.exp2((scores - top) * scale).astype(jnp.bfloat16)
        else:
            parts = []
            for n, bias in enumerate(biases):
                part = (scores[:, n * BLK : (n + 1) * BLK] - top) * scale
                parts.append(jnp.exp2(part if bias is None else part + bias).astype(jnp.bfloat16))
            weights = jnp.concatenate(parts, axis=1)
        value_all = jnp.concatenate(values, axis=0)
        value_ones = jnp.concatenate([value_all, jnp.ones_like(value_all)], axis=1)
        total = jnp.dot(weights, value_ones, preferred_element_type=jnp.float32)
        denominator = total[:, BLK:]
        result = (total[:, :BLK] / denominator).astype(jnp.bfloat16)
        lse = top * scale + jnp.log(denominator) * math.log2(math.e)
        lse_row = jnp.sum(jnp.where(eye, lse, 0.0), axis=0, keepdims=True)
        return result, lse_row

    def hand_back(is_mine, src, dst, lsrc, ldst, row, device, o_sem, l_sem):
        def keep():
            pltpu.make_async_copy(src, dst, o_sem).start()
            pltpu.make_async_copy(lsrc, ldst, l_sem).start()

        def give():
            remote(src, dst, o_send.at[row], o_sem, device).start()
            remote(lsrc, ldst, l_send.at[row], l_sem, device).start()

        if is_mine is False:
            give()
        else:
            pl.when(is_mine)(keep)
            pl.when(jnp.logical_not(is_mine))(give)

    def return_pair(p, j, shift, mine):
        frame = at(*shift)
        there = group_there(*walk(j))
        hand_back(
            mine,
            t_out[p].at[frame],
            t_got[p].at[wide],
            t_lse[p].at[frame],
            t_lgot[p].at[wide],
            2 * p,
            (frame, seq),
            last_o.at[there] if p == NP - 1 else o_recv.at[2 * p],
            last_l.at[there] if p == NP - 1 else l_recv.at[2 * p],
        )

    def over_pairs(first, count, visit):
        def body(step, _):
            ahead, back, mine = two_ways(*walk(first + step))
            visit(first + step, ahead, False)
            visit(first + step, back, mine)
            return 0

        lax.fori_loop(0, count, body, 0)

    def work_pairs(p):
        for n in range(2):
            wait_all(t_in[p][n], t_recv.at[p, n])
        keys, values, queries = t_in[p]

        def visit(j, shift, mine):
            frame = at(*shift)
            first, second, count = decode(tl_s[frame, 0, place_of(wide, p)[0]])
            result, lse = attend(
                queries[frame], (keys[first], keys[second]), (values[first], values[second]), None
            )
            twice = jnp.where(count == 2, 0.0, jnp.where(count == 1, -1.0, DEAD))
            t_out[p][frame] = result
            t_lse[p][frame] = lse + twice
            if p != NP - 2:
                return_pair(p, j, shift, mine)

        if p < NP - 1:
            wait_all(queries, t_recv.at[p, 2])
            over_pairs(0, steps, visit)
            return

        over_pairs(0, steps, lambda j, shift, mine: return_pair(p - 1, j, shift, mine))

        def group(k, _):
            wait_all(queries.at[pl.ds(0, 2 * half)], last_q.at[k])
            over_pairs(k * half, half, visit)
            return 0

        lax.fori_loop(0, NY, group, 0)

    def work_heads(p):
        for n in range(3):
            wait_all(s_in[p][n], s_recv.at[p, n])
        keys, values, queries = s_in[p]

        def body(step, _):
            for u in range(UNROLL):
                i = step * UNROLL + u
                c2, block = i // BPF, (i % BPF + 2 * seq) % BPF
                row = c2 * BPF + block
                first, second, count = decode(sl_s[block, 0, seq * (NP * C2) + p + NP * c2])
                first, second = c2 * BPF + first, c2 * BPF + second
                live_first = jnp.where(count >= 1, 0.0, DEAD)
                live_second = jnp.where(count >= 2, 0.0, DEAD)
                result, lse = attend(
                    queries[row],
                    (keys[row], keys[first], keys[second]),
                    (values[row], values[first], values[second]),
                    (None, live_first, live_second),
                )
                s_out[p][row] = result
                s_lse[p][row] = lse
                home, place = block // 2, block % 2 * (W // 2) + C2 * seq + c2
                hand_back(
                    home == seq,
                    s_out[p].at[row],
                    s_got[p].at[place],
                    s_lse[p].at[row],
                    s_lgot[p].at[place],
                    2 * p + 1,
                    (wide, home),
                    o_recv.at[2 * p + 1],
                    l_recv.at[2 * p + 1],
                )
            return 0

        lax.fori_loop(0, C2 * BPF // UNROLL, body, 0)

    def join(p, w):
        over_time, in_space = t_lgot[p][w], s_lgot[p][w]
        highest = jnp.maximum(over_time, in_space)
        time_weight = jnp.exp2(over_time - highest)
        space_weight = jnp.exp2(in_space - highest)
        share_row = time_weight / (time_weight + space_weight)
        share = jnp.sum(jnp.where(eye, share_row, 0.0), axis=1, keepdims=True)
        space = s_got[p][w].astype(jnp.float32)
        other = t_got[p][w].astype(jnp.float32)
        out_v[p][w] = (space + share * (other - space)).astype(jnp.bfloat16)
        head, block = place_of(w, p)
        pltpu.make_async_copy(out_v[p].at[w], out_ref.at[block, :, column(head)], out_sem.at[0]).start()

    def combine(p):
        wait_all(s_got[p], o_recv.at[2 * p + 1])
        wait_all(s_lgot[p], l_recv.at[2 * p + 1])
        if p < NP - 1:
            wait_all(t_got[p], o_recv.at[2 * p])
            wait_all(t_lgot[p], l_recv.at[2 * p])

            def body(step, _):
                for u in range(UNROLL):
                    join(p, step * UNROLL + u)
                return 0

            lax.fori_loop(0, W // UNROLL, body, 0)
            return

        def group(k, _):
            wait_all(t_got[p].at[pl.ds(0, 2 * half)], last_o.at[k])
            wait_all(t_lgot[p].at[pl.ds(0, 2 * half)], last_l.at[k])
            over_pairs(k * half, half, lambda j, shift, mine: join(p, at(*shift)))
            return 0

        lax.fori_loop(0, NY, group, 0)

    for p in range(NP):
        work_heads(p)
        work_pairs(p)
    for p in range(NP):
        combine(p)

    kept = BPF * C2 - 2 * C2
    for p in range(NP):
        wait_all(out_v[p], out_sem.at[0])
        for n in range(3):
            wait_all(t_in[p][n].at[pl.ds(0, W - 1)], t_send.at[p, n])
            wait_all(s_in[p][n].at[pl.ds(0, kept)], s_send.at[p, n])
        wait_all(t_out[p].at[pl.ds(0, W - 1)], o_send.at[2 * p])
        wait_all(t_lse[p].at[pl.ds(0, W - 1)], l_send.at[2 * p])
        wait_all(s_out[p].at[pl.ds(0, kept)], o_send.at[2 * p + 1])
        wait_all(s_lse[p].at[pl.ds(0, kept)], l_send.at[2 * p + 1])
    wait_all(tl_v.at[pl.ds(0, W - 1)], list_sem.at[1])


def per_device(queries, keys, values, spatial_mask, temporal_mask):
    W, S = lax.axis_size("wide"), lax.axis_size("seq")
    H, frames = spatial_mask.shape[0], temporal_mask.shape[3]
    BPF = spatial_mask.shape[2]
    NP = 2 * H // W
    C2 = H // (S * NP)
    NY = 4 if W >= 16 else 2
    cfg = (W, S, H, NP, C2, W // NY, NY)
    blocks = (2, BLK, H * BLK)
    many = (W, BLK, BLK)
    some = (C2 * BPF, BLK, BLK)
    scratch = (
        [pltpu.VMEM(many, jnp.bfloat16)] * (3 * NP)
        + [pltpu.VMEM(some, jnp.bfloat16)] * (3 * NP)
        + [pltpu.VMEM(many, jnp.bfloat16)] * NP
        + [pltpu.VMEM(some, jnp.bfloat16)] * NP
        + [pltpu.VMEM(many, jnp.bfloat16)] * (2 * NP)
        + [pltpu.VMEM((W, 1, BLK), jnp.float32)] * NP
        + [pltpu.VMEM((C2 * BPF, 1, BLK), jnp.float32)] * NP
        + [pltpu.VMEM((W, 1, BLK), jnp.float32)] * (2 * NP)
        + [pltpu.VMEM(many, jnp.bfloat16)] * NP
        + [pltpu.VMEM((2, 1, frames, H), jnp.int32), pltpu.VMEM((BPF, BPF, H), jnp.int32)]
        + [pltpu.VMEM((rows, 1, H), jnp.int32) for rows in (2, W, BPF)]
        + [pltpu.SMEM((rows, 1, H), jnp.int32) for rows in (W, BPF)]
        + [pltpu.SemaphoreType.DMA((NP, 3))] * 4
        + [pltpu.SemaphoreType.DMA((2 * NP,))] * 4
        + [pltpu.SemaphoreType.DMA((4,)), pltpu.SemaphoreType.DMA((1,))]
        + [pltpu.SemaphoreType.DMA((NY,))] * 3
    )
    by_head = [jnp.transpose(mask, (1, 2, 3, 0)) for mask in (temporal_mask, spatial_mask)]
    anywhere = pl.BlockSpec(memory_space=pltpu.HBM)
    result = pl.pallas_call(
        functools.partial(kernel, cfg),
        out_shape=jax.ShapeDtypeStruct(blocks, jnp.bfloat16),
        in_specs=[anywhere] * 5,
        out_specs=anywhere,
        scratch_shapes=scratch,
        compiler_params=pltpu.CompilerParams(
            collective_id=0, has_side_effects=True, vmem_limit_bytes=56 * 1024 * 1024
        ),
    )(queries.reshape(blocks), keys.reshape(blocks), values.reshape(blocks), *by_head)
    return result.reshape(queries.shape)


def solution(mesh):
    return jax.shard_map(
        per_device,
        mesh=mesh,
        in_specs=(
            P(("wide", "seq"), None),
            P(("wide", "seq"), None),
            P(("wide", "seq"), None),
            P(None, "wide", None, None),
            P(None, None, "wide", None),
        ),
        out_specs=P(("wide", "seq"), None),
        check_vma=False,
    )
```

time: 689 us -> 291 us (0.42); the launches traced: 678 us -> 291 us
  waiting for transfers between devices: 309 us -> 0 us
  Pallas kernels: 0 us -> 287 us
  local copies, waits for them, and re-layouts: 142 us -> 3.88 us
  starting transfers between devices: 62.1 us -> 0 us
  blocking collectives: 60 us -> 0 us
  matrix products: 55.7 us -> 0 us
  other arithmetic: 44.1 us -> 0 us
    all_to_all x5 -> x0, waiting for transfers between devices: 309 us -> none  [the longest x1 211 us: per_device(): lax.all_to_all(outgoing, 'wide', split_axis=0, concat_axis=2, tiled=True)]
    pallas_call x0 -> x1, Pallas kernels: none -> 287 us  [per_device(): pl.pallas_call(functools.partial(kernel, cfg), out_shape=jax.ShapeDtypeSt...]
    all_to_all x5 -> x0, starting transfers between devices: 62.1 us -> none  [the longest x1 37.3 us: per_device(): lax.all_to_all(partial_value.astype(jnp.bfloat16), 'wide', split_axis=2,...]
    all_to_all x1 -> x0, blocking collectives: 60 us -> none  [per_device(): lax.all_to_all(leaving, 'seq', split_axis=0, concat_axis=1, tiled=True)]
    dot_general x8 -> x0, matrix products: 55.7 us -> none  [the longest x4 34.9 us: visit_slot(): jnp.einsum('nqk,nkd->nqd', weights.astype(jnp.bfloat16), value_block, pre...]
    all_to_all x6 -> x0, local copies, waits for them, and re-layouts: 32.9 us -> none  [the longest x1 8.85 us: per_device(): lax.all_to_all(outgoing, 'wide', split_axis=0, concat_axis=2, tiled=True)]
    gather x8 -> x0, local copies, waits for them, and re-layouts: 30.6 us -> none  [the longest x4 18.4 us: visit_slot(): key_block = jnp.take(key_rows, target, axis=0)]
    slice x6 -> x0, local copies, waits for them, and re-layouts: 27.3 us -> none  [the longest x2 11.3 us: per_device(): value_in = incoming[0, :, :, 2 * block_rows:3 * block_rows]]
  transfers between devices with their start and end apart: 5 -> 0, of which waited for: 4 -> 0; matrix products, arithmetic and copies ran while one was open for 14% -> 0% of each run, Pallas kernels for 0% -> 0%
where the time goes in v1:
time: 291 us
  Pallas kernels  287 us (99%)
  local copies, waits for them, and re-layouts  3.88 us (1%)
    pallas_call x1, Pallas kernels, per_device(): pl.pallas_call(functools.partial(kernel, cfg), out_shape=jax.ShapeDtypeSt...  287 us

profile of v1, /device:TPU:32, one launch (start us, length us, event | category | flops | bytes accessed | tf_op | source)
XLA Modules:
  0.0 290.8 jit_solution(5142351423559265999)
XLA Ops:
  0.0 286.9 %shard_map.55 = bf16[2,128,6144]{2,1,0:T(8,128)(2,1)} custom-call(bf16[2,128,6144]{2,1,0:T(8,128)(2,1)} %bitcast.7, bf16[2,128,6144]{2,1,0:T(8,128)(2,1)} %bitcast.8, bf16[2,128,6144]{2,1,0:T(8,128)(2,1)} %bitcast.9, s32[16,1,32,48]{3,2,1,0:T(8,128)} %bitcast.10, s32[1,16,16,48]{3,2,1,0:T(8,128)} %bitcast.11), custom_call_target="tpu_custom_call" | custom-call | tf_op jit(solution)/shard_map/pallas_call | solution.py:427
  286.9 3.9 %copy.7 = bf16[256,6144]{1,0:T(8,128)(2,1)} copy(bf16[256,6144]{1,0:T(8,128)(2,1)} %bitcast.6) | data formatting | bytes 6291456

commit v2 on v1

--- a/solution.py
+++ b/solution.py
@@ -291,10 +291,9 @@
             over_pairs(0, steps, visit)
             return
 
-        over_pairs(0, steps, lambda j, shift, mine: return_pair(p - 1, j, shift, mine))
-
         def group(k, _):
             wait_all(queries.at[pl.ds(0, 2 * half)], last_q.at[k])
+            over_pairs(k * half, half, lambda j, shift, mine: return_pair(p - 1, j, shift, mine))
             over_pairs(k * half, half, visit)
             return 0
 
@@ -391,6 +390,20 @@
         wait_all(s_out[p].at[pl.ds(0, kept)], o_send.at[2 * p + 1])
         wait_all(s_lse[p].at[pl.ds(0, kept)], l_send.at[2 * p + 1])
     wait_all(tl_v.at[pl.ds(0, W - 1)], list_sem.at[1])
+
+
+def copy_out(parts, in_ref, out_ref, held, in_sems, out_sems):
+    rows = in_ref.shape[1] // parts
+    pieces = [(n, pl.ds(k * rows, rows)) for n in range(in_ref.shape[0]) for k in range(parts)]
+    coming = [pltpu.make_async_copy(in_ref.at[p], held.at[p], in_sems.at[i]) for i, p in enumerate(pieces)]
+    going = [pltpu.make_async_copy(held.at[p], out_ref.at[p], out_sems.at[i]) for i, p in enumerate(pieces)]
+    for copy in coming:
+        copy.start()
+    for first, second in zip(coming, going):
+        first.wait()
+        second.start()
+    for copy in going:
+        copy.wait()
 
 
 def per_device(queries, keys, values, spatial_mask, temporal_mask):
@@ -434,6 +447,15 @@
             collective_id=0, has_side_effects=True, vmem_limit_bytes=56 * 1024 * 1024
         ),
     )(queries.reshape(blocks), keys.reshape(blocks), values.reshape(blocks), *by_head)
+    parts = 8
+    result = pl.pallas_call(
+        functools.partial(copy_out, parts),
+        out_shape=jax.ShapeDtypeStruct(blocks, jnp.bfloat16),
+        in_specs=[anywhere],
+        out_specs=anywhere,
+        scratch_shapes=[pltpu.VMEM(blocks, jnp.bfloat16)] + [pltpu.SemaphoreType.DMA((blocks[0] * parts,))] * 2,
+        compiler_params=pltpu.CompilerParams(vmem_limit_bytes=60 * 1024 * 1024),
+    )(result)
     return result.reshape(queries.shape)
 
 

time: 291 us -> 290 us (level)
  local copies, waits for them, and re-layouts: 3.88 us -> 0 us
  Pallas kernels: 287 us -> 290 us
    unnamed x1 -> x0, local copies, waits for them, and re-layouts: 3.88 us -> none
    pallas_call x0 -> x1, Pallas kernels: none -> 3.17 us  [per_device(): pl.pallas_call(functools.partial(copy_out, parts), out_shape=jax.ShapeDty...]
where the time goes in v2:
time: 290 us
  Pallas kernels  290 us (100%)
    pallas_call x1, Pallas kernels, per_device(): pl.pallas_call(functools.partial(kernel, cfg), out_shape=jax.ShapeDtypeSt...  287 us

profile of v2, /device:TPU:32, one launch (start us, length us, event | category | flops | bytes accessed | tf_op | source)
XLA Modules:
  0.0 290.1 jit_solution(14409740377047170785)
XLA Ops:
  0.0 286.9 %shard_map.55.in_ref = bf16[2,128,6144]{2,1,0:T(8,128)(2,1)} custom-call(bf16[2,128,6144]{2,1,0:T(8,128)(2,1)} %bitcast.6, bf16[2,128,6144]{2,1,0:T(8,128)(2,1)} %bitcast.7, bf16[2,128,6144]{2,1,0:T(8,128)(2,1)} %bitcast.8, s32[16,1,32,48]{3,2,1,0:T(8,128)} %bitcast.9, s32[1,16,16,48]{3,2,1,0:T(8,128)} %bitcast.10), custom_call_target="tpu_custom_call" | custom-call | tf_op jit(solution)/shard_map/pallas_call | solution.py:440
  286.9 3.2 %shard_map.56 = bf16[2,128,6144]{2,1,0:T(8,128)(2,1)} custom-call(bf16[2,128,6144]{2,1,0:T(8,128)(2,1)} %shard_map.55.in_ref), custom_call_target="tpu_custom_call" | custom-call | tf_op jit(solution)/shard_map/pallas_call | solution.py:451
